TPU v7x, 256 devices: a whole 4x4x8 slice. The times are simulated.
256 devices in a mesh: head: 16 (over z, x_lo), ctx: 16 (over y, x_hi, core).
Axes of the slice: x: 4 (x_hi: 2, x_lo: 2; x = x_hi * 2 + x_lo), y: 4, z: 8, core: 2. Of those that a mesh axis runs over, the one named last changes fastest.
Arguments:
- query_latent: bfloat16 [1024, 1536], P('ctx'), may hold values from -6 to 6
- w_query_nope: bfloat16 [1536, 16384], P(None, 'head'), may hold values from -0.15625 to 0.15625
- w_query_rope: bfloat16 [1536, 8192], P(None, 'head'), may hold values from -0.15625 to 0.15625
- w_absorb_key: bfloat16 [128, 128, 512], P('head'), may hold values from -0.5 to 0.5
- w_absorb_value: bfloat16 [128, 512, 128], P('head'), may hold values from -0.25 to 0.25
- w_output: bfloat16 [16384, 7168], P('head', 'ctx'), may hold values from -0.046875 to 0.046875
- latent_cache: bfloat16 [32, 1024, 576], P(None, 'ctx'), may hold values from -250 to 250
- block_lists: int32 [64, 48], replicated, may hold values from 0 to 511, as said below
- block_counts: int32 [64], replicated, may hold values from 24 to 48, as said below
- positions: int32 [1024], replicated, may hold values from 1024 to 8191
Outputs:
- attended: bfloat16 [1024, 7168], P('head', 'ctx')
Inputs may be any that keep to these rules, and one draw needn't show every extreme that they name: `block_lists`: entries at or beyond a tile's count are block ids to be ignored. Among a tile's valid entries no block repeats and at most 4 lie in one shard (blocks of equal residue modulo 512 / 32); tile 0 has 4 valid entries in one shard. `block_counts`: tile 0 has 48 valid entries.
All inputs are finite; a program needn't handle non-finite values.
Results may differ from a plain program's by a relative error of at most 0.011.
Values may be sent and summed in bfloat16 or wider, within the bound.
A program may use at most 192 MiB of HBM per device.

v0:
```python
import jax
import jax.numpy as jnp
from jax import lax
from jax.sharding import PartitionSpec as P

LAT = 512
ROPE = 64
NOPE = 128
VDIM = 128
BLK = 64
TILE = 16
MAXB = 48


def rotate(rope_part, token_positions):
    half_width = ROPE // 2
    frequency = 10000.0 ** (-2.0 * jnp.arange(half_width).astype(jnp.float32) / ROPE)
    angles = token_positions.astype(jnp.float32)[:, None] * frequency[None, :]
    cosine = jnp.cos(angles)[:, None, :]
    sine_part = jnp.sin(angles)[:, None, :]
    first_half = rope_part[..., :half_width]
    second_half = rope_part[..., half_width:]
    return jnp.concatenate(
        [
            first_half * cosine - second_half * sine_part,
            first_half * sine_part + second_half * cosine,
        ],
        axis=-1,
    )


def make_queries(query_latent, w_query_nope, w_query_rope, w_absorb_key, token_positions):
    row_count = query_latent.shape[0]
    head_count = w_absorb_key.shape[0]
    nope_part = jnp.dot(query_latent, w_query_nope, preferred_element_type=jnp.float32).astype(
        jnp.bfloat16
    )
    nope_part = nope_part.reshape(row_count, head_count, NOPE)
    latent_part = jnp.einsum(
        "thn,hnl->thl", nope_part, w_absorb_key, preferred_element_type=jnp.float32
    ).astype(jnp.bfloat16)
    rope_part = jnp.dot(query_latent, w_query_rope, preferred_element_type=jnp.float32).reshape(
        row_count, head_count, ROPE
    )
    rope_part = rotate(rope_part, token_positions).astype(jnp.bfloat16)
    return jnp.concatenate([latent_part, rope_part], axis=-1)


def local(
    query_latent,
    w_query_nope,
    w_query_rope,
    w_absorb_key,
    w_absorb_value,
    w_output,
    latent_cache,
    block_lists,
    block_counts,
    positions,
):
    shards = lax.axis_size("ctx")
    my_index = lax.axis_index("ctx")
    tok_dev = query_latent.shape[0]
    tokens = tok_dev * shards
    head_count = w_absorb_key.shape[0]
    most_local = (MAXB + shards - 1) // shards + 1
    own_positions = lax.dynamic_slice_in_dim(positions, my_index * tok_dev, tok_dev)
    own_queries = make_queries(
        query_latent, w_query_nope, w_query_rope, w_absorb_key, own_positions
    )
    queries = lax.all_gather(own_queries, "ctx", axis=0, tiled=True)
    tile_count = tokens // TILE
    tiles_step = 4
    tiled_queries = queries.reshape(
        tile_count // tiles_step, tiles_step, TILE, head_count, LAT + ROPE
    )
    tile_lists = block_lists.reshape(tile_count // tiles_step, tiles_step, MAXB)
    tile_counts = block_counts.reshape(tile_count // tiles_step, tiles_step)
    scale = (NOPE + ROPE) ** (-0.5)

    def local_blocks(tile_list, tile_total):
        slots = jnp.arange(MAXB)
        is_local = (slots < tile_total) & (tile_list % shards == my_index)
        slot_rank = jnp.cumsum(is_local.astype(jnp.int32)) - 1
        chosen = is_local[:, None] & (slot_rank[:, None] == jnp.arange(most_local)[None, :])
        block_index = jnp.sum(jnp.where(chosen, (tile_list // shards)[:, None], 0), axis=0)
        is_live = jnp.any(chosen, axis=0)
        return (block_index, is_live)

    def tile_step(operands):
        step_queries, step_lists, step_counts = operands
        block_index, is_live = jax.vmap(local_blocks)(step_lists, step_counts)
        key_rows = latent_cache[block_index].reshape(tiles_step, most_local * BLK, LAT + ROPE)
        key_live = jnp.repeat(is_live, BLK, axis=1)[:, None, None, :]
        scores = (
            jnp.einsum("gqhc,gkc->gqhk", step_queries, key_rows, preferred_element_type=jnp.float32)
            * scale
        )
        peak_score = jnp.max(jnp.where(key_live, scores, -1e30), axis=-1)
        weights = jnp.where(key_live, jnp.exp(scores - peak_score[..., None]), 0.0).astype(
            jnp.bfloat16
        )
        weight_sum = jnp.sum(weights.astype(jnp.float32), axis=-1)
        numerator = jnp.einsum(
            "gqhk,gkl->gqhl", weights, key_rows[..., :LAT], preferred_element_type=jnp.float32
        )
        return (peak_score, weight_sum, numerator)

    peak_score, weight_sum, numerator = lax.map(tile_step, (tiled_queries, tile_lists, tile_counts))
    peak_score = peak_score.reshape(tokens, head_count)
    weight_sum = weight_sum.reshape(tokens, head_count)
    numerator = numerator.reshape(tokens, head_count, LAT)
    value_weight = w_absorb_value.astype(jnp.float32)
    recv_peak, recv_sum, recv_numerator = (
        lax.all_to_all(peak_score[None], "ctx", split_axis=1, concat_axis=0, tiled=True),
        lax.all_to_all(weight_sum[None], "ctx", split_axis=1, concat_axis=0, tiled=True),
        lax.all_to_all(numerator[None], "ctx", split_axis=1, concat_axis=0, tiled=True),
    )
    global_peak = jnp.max(recv_peak, axis=0)
    shard_weight = jnp.exp(recv_peak - global_peak[None])
    denominator = jnp.sum(shard_weight * recv_sum, axis=0)
    mixed_latent = (
        jnp.sum(shard_weight[..., None] * recv_numerator, axis=0) / denominator[..., None]
    )
    own_values = jnp.einsum(
        "thl,hlv->thv", mixed_latent, value_weight, precision=lax.Precision.HIGHEST
    )
    own_values = own_values.astype(jnp.bfloat16).reshape(tok_dev, head_count * VDIM)
    values = lax.all_gather(own_values, "ctx", axis=0, tiled=True)
    attended_out = lax.psum_scatter(
        jnp.dot(values, w_output, preferred_element_type=jnp.float32),
        "head",
        scatter_dimension=0,
        tiled=True,
    )
    return attended_out.astype(jnp.bfloat16)


def solution(mesh):
    in_specs = (
        P("ctx", None),
        P(None, "head"),
        P(None, "head"),
        P("head", None, None),
        P("head", None, None),
        P("head", "ctx"),
        P(None, "ctx", None),
        P(),
        P(),
        P(),
    )
    out_specs = P("head", "ctx")
    return jax.shard_map(local, mesh=mesh, in_specs=in_specs, out_specs=out_specs, check_vma=False)
```

profile of v0, /device:TPU:24, one launch (start us, length us, event | category | flops | bytes accessed | tf_op | source)
XLA Modules:
  0.0 590.1 jit_solution(48270103532917880)
XLA Ops:
  6.6 2.0 fusion.18
  9.6 1.6 fusion.10
  12.2 1.5 fusion.9
  16.0 87.6 %all-gather.3.cloned.1.call-done = bf16[1024,8,576]{2,0,1:T(8,128)(2,1)} async-done(((bf16[64,8,576]{2,0,1:T(8,128)(2,1)}), bf16[1024,8,576]{2,0,1:T(8,128)(2,1)}) %all-gather.3.cloned.1.call-update) | async-done | bytes 9437200 | tf_op jit(solution)/shard_map/all_gather | solution.py:71
  103.6 120.8 %while.17 = (s32[]{:T(128)}, f32[16,4,16,8]{3,2,1,0:T(8,128)S(1)}, f32[16,4,16,8]{3,2,1,0:T(8,128)}, f32[16,4,16,8,512]{4,3,2,1,0:T(8,128)}, s32[16,4]{1,0:T(8,1...) while((s32[]{:T(128)}, f32[16,4,16,8]{3,2,1,0:T(8,128)S(1)}, ...), condition=%wide.region_6.7_spmd, body=%wide.region_0.6_spmd.sunk | while | flops 286674816 | bytes 9169365 | solution.py:109
  104.2 2.5 gather_fusion
  107.1 1.2 constant_dynamic-slice_fusion.4
  109.0 1.4 fusion.38
  111.8 2.5 gather_fusion
  114.6 1.2 constant_dynamic-slice_fusion.4
  116.5 1.4 fusion.38
  119.3 2.5 gather_fusion
  122.2 1.2 constant_dynamic-slice_fusion.4
  124.1 1.3 fusion.38
  126.9 2.5 gather_fusion
  129.8 1.2 constant_dynamic-slice_fusion.4
  131.6 1.3 fusion.38
  134.4 2.5 gather_fusion
  137.3 1.2 constant_dynamic-slice_fusion.4
  139.2 1.3 fusion.38
  142.0 2.5 gather_fusion
  144.8 1.2 constant_dynamic-slice_fusion.4
  146.7 1.4 fusion.38
  149.5 2.5 gather_fusion
  152.4 1.2 constant_dynamic-slice_fusion.4
  154.3 1.4 fusion.38
  157.1 2.5 gather_fusion
  159.9 1.2 constant_dynamic-slice_fusion.4
  161.8 1.3 fusion.38
  164.6 2.5 gather_fusion
  167.5 1.2 constant_dynamic-slice_fusion.4
  169.3 1.4 fusion.38
  172.2 2.5 gather_fusion
  175.1 1.2 constant_dynamic-slice_fusion.4
  177.0 1.3 fusion.38
  179.8 2.5 gather_fusion
  182.6 1.2 constant_dynamic-slice_fusion.4
  184.5 1.3 fusion.38
  187.3 2.5 gather_fusion
  190.1 1.2 constant_dynamic-slice_fusion.4
  192.0 1.3 fusion.38
  194.8 2.5 gather_fusion
  197.7 1.2 constant_dynamic-slice_fusion.4
  199.5 1.4 fusion.38
  202.4 2.5 gather_fusion
  207.1 1.3 fusion.38
  209.9 2.5 gather_fusion
  212.8 1.2 constant_dynamic-slice_fusion.4
  214.7 1.3 fusion.38
  217.5 2.5 gather_fusion
  222.2 1.4 fusion.38
  225.0 2.0 reduce.2
  227.9 5.7 all-to-all-start
  233.6 3.0 reduce
  237.0 2.3 all-to-all-done
  239.2 10.4 %all_to_all.36 = f32[16,1,512]{2,1,0:T(1,128)S(1)} all-to-all(f32[16,1,512]{2,1,0:T(1,128)S(1)} %reshape.283), channel_id=1, replica_groups=mesh['head'=16,'ctx'=16] {'ctx'}, dimensions={0} | all-to-all | bytes 65536 | tf_op jit(solution)/shard_map/all_to_all | solution.py:116
  249.6 7.0 %all-to-all-start.1 = ((f32[1,1024,8,512]{3,2,0,1:T(8,128)}), f32[1,1024,8,512]{3,2,0,1:T(8,128)}, u32[]{:S(2)}, u32[]{:S(2)}) async-start(f32[1,1024,8,512]{3,2,0,1:T(8,128)} %bitcast.110), calls=%async_computation.1 | async-start | bytes 33554432 | tf_op jit(solution)/shard_map/all_to_all | solution.py:117
  260.1 181.7 %all-to-all-done.1 = f32[1,1024,8,512]{3,2,0,1:T(8,128)} async-done(((f32[1,1024,8,512]{3,2,0,1:T(8,128)}), f32[1,1024,8,512]{3,2,0,1:T(8,128)}, u32[]{:S(2)}, u32[]{:S(2)}) %all-to-all-start.1) | async-done | bytes 16777248 | tf_op jit(solution)/shard_map/all_to_all | solution.py:117
  441.8 6.8 %multiply_reduce_fusion = f32[64,8,512]{2,1,0:T(8,128)S(1)} fusion(f32[16,64,8,512]{3,2,1,0:T(8,128)} %bitcast.17, f32[16,64,8]{2,1,0:T(8,128)S(1)} %get-tuple-element.213), kind=kLoop, calls=%fused_computation.36 | loop fusion | flops 8126464 | bytes 17858560 | tf_op jit(solution)/shard_map/reduce_sum | solution.py:123
  449.8 1.2 fusion.11
  451.7 51.2 %all-gather.5.cloned.1.call-done = bf16[1024,1024]{1,0:T(8,128)(2,1)} async-done(((bf16[64,1024]{1,0:T(8,128)(2,1)}), bf16[1024,1024]{1,0:T(8,128)(2,1)}) %all-gather.5.cloned.1.call-update) | async-done | bytes 2097168 | tf_op jit(solution)/shard_map/all_gather | solution.py:129
  502.9 4.5 fusion.19
  507.5 74.5 %reduce-scatter.2.cloned.1.call-done = f32[64,448]{1,0:T(8,128)} async-done(((f32[1024,448]{1,0:T(8,128)}), f32[64,448]{1,0:T(8,128)}) %reduce-scatter.2.cloned.1.call-update) | async-done | bytes 114704 | tf_op jit(solution)/shard_map/reduce_scatter | solution.py:130
  582.0 1.5 convert_element_type.62
  (283 shorter events, 53.3 us)
Async XLA Ops:
  6.5 3.0 copy-start
  6.5 97.1 %all-gather.3.cloned.1.call-start = ((), (), s32[]{:S(2)}) async-start(), calls=%async_computation.4 | async-start | bytes 11141120 | tf_op jit(solution)/shard_map/all_gather | solution.py:71
  9.6 4.2 copy-start.3
  12.2 3.7 copy-start.4
  12.2 3.7 copy-start.5
  227.9 11.3 %all-to-all-start = ((f32[16,1,512]{2,1,0:T(1,128)}), f32[16,1,512]{2,1,0:T(1,128)S(1)}, u32[]{:S(2)}, u32[]{:S(2)}) async-start(f32[16,1,512]{2,1,0:T(1,128)} %reshape.281), calls=%async_computation | async-start | bytes 65536 | tf_op jit(solution)/shard_map/all_to_all | solution.py:115
  249.6 192.2 %all-to-all-start.1 = ((f32[1,1024,8,512]{3,2,0,1:T(8,128)}), f32[1,1024,8,512]{3,2,0,1:T(8,128)}, u32[]{:S(2)}, u32[]{:S(2)}) async-start(f32[1,1024,8,512]{3,2,0,1:T(8,128)} %bitcast.110), calls=%async_computation.1 | async-start | bytes 33554432 | tf_op jit(solution)/shard_map/all_to_all | solution.py:117
  256.6 246.3 %all-gather.5.cloned.1.call-start = ((), (), s32[]{:S(2)}) async-start(), calls=%async_computation.5 | async-start | bytes 2228224 | tf_op jit(solution)/shard_map/all_gather | solution.py:129
  448.6 1.2 copy-start.2
  451.7 130.3 %reduce-scatter.2.cloned.1.call-start = ((), (), s32[]{:S(2)}) async-start(), calls=%async_computation.6 | async-start | bytes 2228224 | tf_op jit(solution)/shard_map/reduce_scatter | solution.py:130
  502.9 80.6 %copy-start.1 = (bf16[1536,1024]{1,0:T(8,128)(2,1)S(1)}, bf16[1536,1024]{1,0:T(8,128)(2,1)}, u32[]{:S(2)}) copy-start(bf16[1536,1024]{1,0:T(8,128)(2,1)} %param.13) | copy-start | bytes 9437188
Sparse Core Ops, SparseCore 0:
  15.9 87.6 all-gather.2
  451.8 51.0 all-gather.4
  507.6 74.3 reduce-scatter.1
where the time goes:
time: 592 us; the launch traced here: 590 us
  waiting for transfers between devices  397 us (67%)
  local copies, waits for them, and re-layouts  79.1 us (13%)
  matrix products  44.1 us (7%)
  other arithmetic  32.4 us (5%)
  between operations  13.3 us (2%)
  starting transfers between devices  12.9 us (2%)
  blocking collectives  10.4 us (2%)
    all_to_all x1, waiting for transfers between devices, local(): lax.all_to_all(numerator[None], 'ctx', split_axis=1, concat_axis=0, tiled...  182 us
    all_gather x1, waiting for transfers between devices, local(): queries = lax.all_gather(own_queries, 'ctx', axis=0, tiled=True)  87.6 us
    reduce_scatter x1, waiting for transfers between devices, local(): lax.psum_scatter(jnp.dot(values, w_output, preferred_element_type=jnp.flo...  74.5 us
    all_gather x1, waiting for transfers between devices, local(): values = lax.all_gather(own_values, 'ctx', axis=0, tiled=True)  51.2 us
    gather x16, local copies, waits for them, and re-layouts, tile_step(): latent_cache[block_index].reshape(tiles_step, most_local * BLK, LAT + ROPE)  40.5 us
    dot_general x16, matrix products, tile_step(): jnp.einsum('gqhk,gkl->gqhl', weights, key_rows[..., :LAT], preferred_elem...  21.7 us
    dynamic_slice x16, local copies, waits for them, and re-layouts, local(): lax.map(tile_step, (tiled_queries, tile_lists, tile_counts))  18.4 us
  transfers between devices with their start and end apart: 5, of which 5 were waited for; matrix products, arithmetic and copies ran while one was open for 1% of the time, Pallas kernels for 0%

commit v1 on v0

v1 whole, which is shorter than its diff:
```python
import functools

import jax
import jax.numpy as jnp
import numpy as np
from jax import lax
from jax.experimental import pallas as pl
from jax.experimental.pallas import tpu as pltpu
from jax.sharding import PartitionSpec as P

LAT = 512
ROPE = 64
NOPE = 128
VDIM = 128
BLK = 64
TILE = 16
LMAX = 4
NEG = -1e30
LOG2E = 1.4426950408889634
MESH = pl.DeviceIdType.MESH
F32 = jnp.float32
BF16 = jnp.bfloat16


def dot_nt(a, b):
    return lax.dot_general(a, b, (((1,), (1,)), ((), ())), preferred_element_type=F32)


def dot_nn(a, b):
    return jnp.dot(a, b, preferred_element_type=F32)


def kernel(
    sizes,
    ql_hbm, wq_hbm, wr_hbm, wk_hbm, wv_hbm, wo_hbm, cache_hbm,
    lists_ref, counts_ref, pos_ref, freq_ref,
    out_ref,
    ql, wq, wr, wk, wv, wo, cache, rope_key,
    listbuf, scal, scal_smem, posbuf,
    qsend, qrecv, qabs, kstage, nabs,
    psend, precv, ssend, srecv, coef, vall, osend, orecv,
    in_sem, cache_sem, scal_sem,
    q_ss, q_rs, p_ss, p_rs, s_ss, s_rs, v_ss, v_rs, f_ss, f_rs, o_ss, o_rs,
):
    n_ctx, n_head, heads, tok, blocks, maxb, tiles = sizes
    peers = n_ctx // 2
    me_h = lax.axis_index("head")
    me_c = lax.axis_index("ctx")
    me8 = me_c // 2
    core = me_c % 2
    sibling = me8 * 2 + (1 - core)
    nope_w = heads * NOPE
    rope_w = heads * ROPE
    tiles_src = tok // TILE
    rows = heads * TILE
    keys = 2 * LMAX * BLK

    def same_core(offset):
        return (me8 + offset) % peers

    loads = [
        pltpu.make_async_copy(ql_hbm, ql, in_sem.at[0]),
        pltpu.make_async_copy(wq_hbm, wq, in_sem.at[1]),
        pltpu.make_async_copy(wr_hbm, wr, in_sem.at[2]),
        pltpu.make_async_copy(wk_hbm, wk, in_sem.at[3]),
        pltpu.make_async_copy(
            cache_hbm, cache.at[pl.ds(core * blocks, blocks)], in_sem.at[4]
        ),
        pltpu.make_async_copy(wv_hbm, wv, in_sem.at[5]),
        pltpu.make_async_copy(wo_hbm, wo, in_sem.at[6]),
    ]
    for load in loads:
        load.start()

    barrier = pltpu.get_barrier_semaphore()

    def greet_ctx(offset, carry):
        pl.semaphore_signal(
            barrier, inc=1, device_id=(me_h, same_core(offset) * 2 + core), device_id_type=MESH
        )
        return carry

    def greet_head(offset, carry):
        pl.semaphore_signal(
            barrier, inc=1, device_id=((me_h + offset) % n_head, me_c), device_id_type=MESH
        )
        return carry

    pl.semaphore_signal(barrier, inc=1, device_id=(me_h, sibling), device_id_type=MESH)
    lax.fori_loop(1, peers, greet_ctx, 0)
    lax.fori_loop(1, n_head, greet_head, 0)

    pos_row = pos_ref[pl.ds(me8, 1), :].astype(F32)
    posbuf[...] = jnp.transpose(jnp.broadcast_to(pos_row, (128, 128)))
    pos_col = posbuf[pl.ds(pl.multiple_of(core * tok, tok), tok), :]
    angle = pos_col * freq_ref[...]
    cosine = jnp.cos(angle)
    lane = lax.broadcasted_iota(jnp.int32, (tok, 128), 1)
    first_half = (lane % ROPE) < (ROPE // 2)
    sine = jnp.where(first_half, -jnp.sin(angle), jnp.sin(angle))

    loads[0].wait()
    loads[1].wait()
    latent = ql[...]
    chunk = 512
    for start in range(0, nope_w, chunk):
        qsend[:, start : start + chunk] = dot_nn(latent, wq[:, start : start + chunk]).astype(BF16)
    loads[2].wait()
    rope_part = dot_nn(latent, wr[...])
    for start in range(0, rope_w, 128):
        part = rope_part[:, start : start + 128]
        swapped = jnp.where(
            first_half,
            pltpu.roll(part, 128 - ROPE // 2, 1),
            pltpu.roll(part, ROPE // 2, 1),
        )
        qsend[:, nope_w + start : nope_w + start + 128] = (
            part * cosine + swapped * sine
        ).astype(BF16)

    pl.semaphore_wait(barrier, peers - 1 + 1 + n_head - 1)

    def q_copy(offset, slot):
        return pltpu.make_async_remote_copy(
            src_ref=qsend,
            dst_ref=qrecv.at[slot],
            send_sem=q_ss.at[offset],
            recv_sem=q_rs.at[slot],
            device_id=(me_h, same_core(offset) * 2 + core),
            device_id_type=MESH,
        )

    def q_start(offset, carry):
        q_copy(offset, me8).start()
        return carry

    lax.fori_loop(1, peers, q_start, 0)

    cache_copy = pltpu.make_async_remote_copy(
        src_ref=cache_hbm,
        dst_ref=cache.at[pl.ds(core * blocks, blocks)],
        send_sem=cache_sem.at[0],
        recv_sem=cache_sem.at[1],
        device_id=(me_h, sibling),
        device_id_type=MESH,
    )
    cache_copy.start()
    cache_in = pltpu.make_async_remote_copy(
        src_ref=cache_hbm,
        dst_ref=cache.at[pl.ds((1 - core) * blocks, blocks)],
        send_sem=cache_sem.at[0],
        recv_sem=cache_sem.at[1],
        device_id=(me_h, sibling),
        device_id_type=MESH,
    )

    own_q = pltpu.make_async_copy(qsend, qrecv.at[me8], in_sem.at[7])
    own_q.start()

    listbuf[...] = jnp.zeros_like(listbuf)
    listbuf[0:tiles, 0:maxb] = lists_ref[...]
    listbuf[...] = jnp.transpose(listbuf[...])
    counts = counts_ref[...]
    zero = jnp.zeros((1, tiles), jnp.int32)
    found = [zero, zero]
    index = [[zero] * LMAX, [zero] * LMAX]
    for slot in range(maxb):
        entry = listbuf[slot : slot + 1, 0:tiles]
        shard = entry % n_ctx
        local = entry // n_ctx
        valid = counts > slot
        for e in range(2):
            here = valid & (shard == me8 * 2 + e)
            for j in range(LMAX):
                index[e][j] = jnp.where(here & (found[e] == j), local + e * blocks, index[e][j])
            found[e] = found[e] + jnp.where(here, 1, 0)
    scal[...] = jnp.zeros_like(scal)
    for e in range(2):
        for j in range(LMAX):
            scal[e * LMAX + j : e * LMAX + j + 1, 0:tiles] = index[e][j]
        scal[2 * LMAX + e : 2 * LMAX + e + 1, 0:tiles] = found[e]
    scal_copy = pltpu.make_async_copy(scal, scal_smem, scal_sem)
    scal_copy.start()
    scal_copy.wait()

    loads[4].wait()
    cache_in.wait_recv()

    def double_key(b, carry):
        part = cache[b, :, LAT : LAT + ROPE]
        rope_key[b] = jnp.concatenate([part, part], axis=1)
        return carry

    lax.fori_loop(0, 2 * blocks, double_key, 0)

    loads[3].wait()
    loads[5].wait()
    own_q.wait()

    half_lane = lax.broadcasted_iota(jnp.int32, (1, 128), 1)
    half_mask = [
        (half_lane < ROPE).astype(F32).astype(BF16),
        (half_lane >= ROPE).astype(F32).astype(BF16),
    ]
    key_lane = lax.broadcasted_iota(jnp.int32, (1, keys), 1)
    key_slot = key_lane // BLK
    stat_lane = lax.broadcasted_iota(jnp.int32, (rows, 128), 1)
    scale = LOG2E * (NOPE + ROPE) ** (-0.5)

    def p_copy(offset, src_slot, slot):
        return pltpu.make_async_remote_copy(
            src_ref=psend.at[src_slot],
            dst_ref=precv.at[slot],
            send_sem=p_ss.at[offset],
            recv_sem=p_rs.at[slot],
            device_id=(me_h, same_core(offset) * 2 + core),
            device_id_type=MESH,
        )

    def s_copy(offset, src_slot, slot):
        return pltpu.make_async_remote_copy(
            src_ref=ssend.at[src_slot],
            dst_ref=srecv.at[slot],
            send_sem=s_ss.at[offset],
            recv_sem=s_rs.at[slot],
            device_id=(me_h, same_core(offset) * 2 + core),
            device_id_type=MESH,
        )

    def attend(src):
        for h in range(heads):
            nope = qrecv[src, :, h * NOPE : (h + 1) * NOPE]
            qabs[h, :, 0:LAT] = dot_nn(nope, wk[h]).astype(BF16)
            pair = qrecv[src, :, nope_w + (h // 2) * 128 : nope_w + (h // 2) * 128 + 128]
            qabs[h, :, LAT : LAT + 128] = pair * half_mask[h % 2]
        stats = jnp.zeros((rows, 128), F32)
        for i in range(tiles_src):
            tile = (src * 2 + core) * tiles_src + i
            for j in range(2 * LMAX):
                block = scal_smem[j, tile]
                kstage[i, j * BLK : (j + 1) * BLK, 0:LAT] = cache[block, :, 0:LAT]
                kstage[i, j * BLK : (j + 1) * BLK, LAT : LAT + 128] = rope_key[block]
            live_even = scal_smem[2 * LMAX, tile]
            live_odd = scal_smem[2 * LMAX + 1, tile]
            limit = jnp.where(key_slot < LMAX, live_even, live_odd + LMAX)
            bias = jnp.where(key_slot < limit, 0.0, NEG)
            query = qabs[:, i * TILE : (i + 1) * TILE, :].reshape(rows, LAT + 128)
            score = dot_nt(query, kstage[i]) * scale + bias
            peak = jnp.max(score, axis=1, keepdims=True)
            weight = jnp.exp2(score - peak)
            total = jnp.sum(weight, axis=1, keepdims=True)
            number = dot_nn(weight.astype(BF16), kstage[i, :, 0:LAT])
            nabs[:, i * TILE : (i + 1) * TILE, :] = number.astype(BF16).reshape(heads, TILE, LAT)
            stats = jnp.where(stat_lane == i, peak, stats)
            stats = jnp.where(stat_lane == tiles_src + i, total, stats)
        for h in range(heads):
            psend[src, h] = dot_nn(nabs[h], wv[h]).astype(BF16)
        ssend[src] = jnp.transpose(stats)[0 : 2 * tiles_src, :]

    attend(me8)

    def attend_peer(offset, carry):
        src = same_core(offset)
        q_copy(offset, src).wait_recv()
        attend(src)
        p_copy(offset, src, me8).start()
        s_copy(offset, src, me8).start()
        return carry

    lax.fori_loop(1, peers, attend_peer, 0)

    own_p = pltpu.make_async_copy(psend.at[me8], precv.at[me8], in_sem.at[8])
    own_s = pltpu.make_async_copy(ssend.at[me8], srecv.at[me8], in_sem.at[9])
    own_p.start()
    own_s.start()
    own_p.wait()
    own_s.wait()

    def p_wait(offset, carry):
        src = same_core(offset)
        s_copy(offset, src, src).wait_recv()
        p_copy(offset, src, src).wait_recv()
        return carry

    lax.fori_loop(1, peers, p_wait, 0)

    peaks = srecv[:, 0:tiles_src, :]
    sums = srecv[:, tiles_src : 2 * tiles_src, :]
    top = jnp.max(peaks, axis=0, keepdims=True)
    share = jnp.exp2(peaks - top)
    share = share / jnp.sum(share * sums, axis=0, keepdims=True)
    coef[...] = jnp.zeros_like(coef)
    for src in range(peers):
        coef[src * tiles_src : (src + 1) * tiles_src, :] = share[src]
    coef_t = jnp.transpose(coef[...])
    own = vall.at[me_c]
    for i in range(tiles_src):
        mixed = jnp.zeros((rows, VDIM), F32)
        for src in range(peers):
            column = coef_t[:, src * tiles_src + i : src * tiles_src + i + 1]
            part = precv[src, :, i * TILE : (i + 1) * TILE, :].astype(F32)
            mixed = mixed + column * part.reshape(rows, VDIM)
        mixed = mixed.astype(BF16).reshape(heads, TILE, VDIM)
        for h in range(heads):
            own[i * TILE : (i + 1) * TILE, h * VDIM : (h + 1) * VDIM] = mixed[h]

    def v_copy(offset, slot):
        return pltpu.make_async_remote_copy(
            src_ref=vall.at[me_c],
            dst_ref=vall.at[slot],
            send_sem=v_ss.at[offset],
            recv_sem=v_rs.at[slot // 2],
            device_id=(me_h, same_core(offset) * 2 + core),
            device_id_type=MESH,
        )

    def f_copy(offset, slot):
        return pltpu.make_async_remote_copy(
            src_ref=vall.at[slot],
            dst_ref=vall.at[slot],
            send_sem=f_ss.at[offset],
            recv_sem=f_rs.at[slot // 2],
            device_id=(me_h, sibling),
            device_id_type=MESH,
        )

    def o_copy(block, slot):
        return pltpu.make_async_remote_copy(
            src_ref=osend.at[block],
            dst_ref=orecv.at[slot],
            send_sem=o_ss.at[block],
            recv_sem=o_rs.at[slot],
            device_id=(block, me_c),
            device_id_type=MESH,
        )

    def v_start(offset, carry):
        v_copy(offset, me_c).start()
        return carry

    lax.fori_loop(1, peers, v_start, 0)
    f_copy(0, me_c).start()
    loads[6].wait()

    def project(block):
        osend[block] = dot_nn(vall[block], wo[...]).astype(BF16)

        @pl.when(block != me_h)
        def _():
            o_copy(block, me_h).start()

    project(me_c)

    def project_pair(offset, carry):
        src = same_core(offset)
        other = src * 2 + (1 - core)

        @pl.when(offset != 0)
        def _():
            v_copy(offset, src * 2 + core).wait_recv()
            f_copy(offset, src * 2 + core).start()
            project(src * 2 + core)

        f_copy(offset, other).wait_recv()
        project(other)
        return carry

    lax.fori_loop(0, peers, project_pair, 0)

    total = osend[me_h].astype(F32)

    def add_head(offset, total):
        src = (me_h + offset) % n_head
        o_copy(src, src).wait_recv()
        return total + orecv[src].astype(F32)

    total = lax.fori_loop(1, n_head, add_head, total)
    out_ref[...] = total.astype(BF16)

    cache_copy.wait_send()

    def drain_ctx(offset, carry):
        src = same_core(offset)
        q_copy(offset, me8).wait_send()
        p_copy(offset, src, me8).wait_send()
        s_copy(offset, src, me8).wait_send()
        v_copy(offset, me_c).wait_send()
        return carry

    lax.fori_loop(1, peers, drain_ctx, 0)

    def drain_sibling(offset, carry):
        f_copy(offset, same_core(offset) * 2 + core).wait_send()
        return carry

    lax.fori_loop(0, peers, drain_sibling, 0)

    def drain_head(offset, carry):
        o_copy((me_h + offset) % n_head, me_h).wait_send()
        return carry

    lax.fori_loop(1, n_head, drain_head, 0)


def local(
    n_ctx, n_head,
    query_latent, w_query_nope, w_query_rope, w_absorb_key, w_absorb_value, w_output,
    latent_cache, block_lists, block_counts, positions,
):
    tok, q_lat = query_latent.shape
    heads = w_absorb_key.shape[0]
    blocks = latent_cache.shape[0]
    tiles, maxb = block_lists.shape
    cols = w_output.shape[1]
    peers = n_ctx // 2
    tiles_src = tok // TILE
    nope_w = heads * NOPE
    rope_w = heads * ROPE
    rows = heads * TILE
    keys = 2 * LMAX * BLK
    half = ROPE // 2
    frequency = 10000.0 ** (-2.0 * np.arange(half, dtype=np.float64) / ROPE)
    frequency = np.tile(frequency.astype(np.float32), 128 // half)[None, :]
    sizes = (n_ctx, n_head, heads, tok, blocks, maxb, tiles)
    hbm = pl.BlockSpec(memory_space=pl.ANY)
    vmem = pl.BlockSpec(memory_space=pltpu.VMEM)
    dma = pltpu.SemaphoreType.DMA
    return pl.pallas_call(
        functools.partial(kernel, sizes),
        out_shape=jax.ShapeDtypeStruct((tok, cols), BF16),
        in_specs=[hbm] * 7 + [vmem] * 4,
        out_specs=vmem,
        scratch_shapes=[
            pltpu.VMEM((tok, q_lat), BF16),
            pltpu.VMEM((q_lat, nope_w), BF16),
            pltpu.VMEM((q_lat, rope_w), BF16),
            pltpu.VMEM((heads, NOPE, LAT), BF16),
            pltpu.VMEM((heads, LAT, VDIM), BF16),
            pltpu.VMEM((heads * VDIM, cols), BF16),
            pltpu.VMEM((2 * blocks, BLK, LAT + ROPE), BF16),
            pltpu.VMEM((2 * blocks, BLK, 128), BF16),
            pltpu.VMEM((128, 128), jnp.int32),
            pltpu.VMEM((16, 128), jnp.int32),
            pltpu.SMEM((16, 128), jnp.int32),
            pltpu.VMEM((128, 128), F32),
            pltpu.VMEM((tok, nope_w + rope_w), BF16),
            pltpu.VMEM((peers, tok, nope_w + rope_w), BF16),
            pltpu.VMEM((heads, tok, LAT + 128), BF16),
            pltpu.VMEM((tiles_src, keys, LAT + 128), BF16),
            pltpu.VMEM((heads, tok, LAT), BF16),
            pltpu.VMEM((peers, heads, tok, VDIM), BF16),
            pltpu.VMEM((peers, heads, tok, VDIM), BF16),
            pltpu.VMEM((peers, 2 * tiles_src, 128), F32),
            pltpu.VMEM((peers, 2 * tiles_src, 128), F32),
            pltpu.VMEM((128, 128), F32),
            pltpu.VMEM((n_ctx, tok, nope_w), BF16),
            pltpu.VMEM((n_head, tok, cols), BF16),
            pltpu.VMEM((n_head, tok, cols), BF16),
            dma((10,)),
            dma((2,)),
            dma(()),
            dma((peers,)),
            dma((peers,)),
            dma((peers,)),
            dma((peers,)),
            dma((peers,)),
            dma((peers,)),
            dma((peers,)),
            dma((peers,)),
            dma((peers,)),
            dma((peers,)),
            dma((n_head,)),
            dma((n_head,)),
        ],
        compiler_params=pltpu.CompilerParams(
            collective_id=0, has_side_effects=True, vmem_limit_bytes=48 * 1024 * 1024
        ),
    )(
        query_latent, w_query_nope, w_query_rope, w_absorb_key, w_absorb_value, w_output,
        latent_cache, block_lists, block_counts.reshape(1, tiles),
        positions.reshape(positions.shape[0] // 128, 128), jnp.asarray(frequency),
    )


def solution(mesh):
    in_specs = (
        P("ctx", None),
        P(None, "head"),
        P(None, "head"),
        P("head", None, None),
        P("head", None, None),
        P("head", "ctx"),
        P(None, "ctx", None),
        P(),
        P(),
        P(),
    )
    run = functools.partial(local, mesh.shape["ctx"], mesh.shape["head"])
    return jax.shard_map(
        run, mesh=mesh, in_specs=in_specs, out_specs=P("head", "ctx"), check_vma=False
    )
```

time: 592 us -> 113 us (0.19)
  the two profiles are of different devices: /device:TPU:24 before, /device:TPU:10 now
where the time goes in v1:
time: 113 us
  Pallas kernels  105 us (93%)
  local copies, waits for them, and re-layouts  8.4 us (7%)
    pallas_call x1, Pallas kernels, local(): pl.pallas_call(functools.partial(kernel, sizes), out_shape=jax.ShapeDtype...  105 us
    unnamed x17, local copies, waits for them, and re-layouts  8.4 us

profile of v1, /device:TPU:10, one launch (start us, length us, event | category | flops | bytes accessed | tf_op | source)
XLA Modules:
  0.0 113.1 jit_solution(18147591821296476432)
XLA Ops:
  0.0 0.0 copy-start
  0.0 0.9 copy.13.lists_ref
  0.9 1.5 %copy.12.wo_hbm = bf16[1024,448]{1,0:T(8,128)(2,1)S(1)} copy(bf16[1024,448]{0,1:T(8,128)(2,1)} %param.16) | data formatting | bytes 1835008 | tf_op args[5]
  2.4 0.0 copy-done
  2.4 0.0 copy-start.1
  2.4 1.2 %copy-done.1 = bf16[8,128,512]{2,1,0:T(8,128)(2,1)S(1)} copy-done((bf16[8,128,512]{2,1,0:T(8,128)(2,1)S(1)}, bf16[8,128,512]{2,1,0:T(8,128)(2,1)}, u32[]{:S(2)}) %copy-start.1) | copy-done | bytes 1048600
  3.6 0.0 copy-start.2
  3.6 1.2 %copy-done.2 = bf16[8,512,128]{2,1,0:T(8,128)(2,1)S(1)} copy-done((bf16[8,512,128]{2,1,0:T(8,128)(2,1)S(1)}, bf16[8,512,128]{2,1,0:T(8,128)(2,1)}, u32[]{:S(2)}) %copy-start.2) | copy-done | bytes 1048600
  4.9 0.0 copy-start.3
  4.9 0.9 copy-done.3
  5.8 0.0 copy-start.4
  5.8 0.7 copy-done.4
  6.5 0.0 copy-start.5
  6.5 0.7 copy-done.5
  7.1 0.0 copy-start.6
  7.1 0.7 copy-done.6
  7.8 104.7 %shard_map.109 = bf16[64,448]{1,0:T(8,128)(2,1)S(1)} custom-call(bf16[64,1536]{1,0:T(8,128)(2,1)S(1)} %copy-done.3, bf16[1536,1024]{1,0:T(8,128)(2,1)} %wq_hbm.1, bf16[1536,512]{1,0:T(8,128)(2,1)S(1)} %copy-done, bf16[8,128,512]{2,1,0:T(8,128)(2,1)S(1)} %copy-done.1, bf16[8,512,128]{2,1,0:T(8,128)(2,1)S(1)} %copy-done.2, bf16[1024,448]{1,0:T(8,128)(2,1)S(1)} %copy.12.wo_hbm, ...), custom_call_target="tpu_custom_call" | custom-call | tf_op jit(solution)/shard_map/pallas_call | solution.py:428
  112.5 0.6 copy.15
Async XLA Ops:
  0.0 2.4 %copy-start = (bf16[1536,512]{1,0:T(8,128)(2,1)S(1)}, bf16[1536,512]{1,0:T(8,128)(2,1)}, u32[]{:S(2)}) copy-start(bf16[1536,512]{1,0:T(8,128)(2,1)} %wr_hbm.1) | copy-start | bytes 4718596
  2.4 1.2 %copy-start.1 = (bf16[8,128,512]{2,1,0:T(8,128)(2,1)S(1)}, bf16[8,128,512]{2,1,0:T(8,128)(2,1)}, u32[]{:S(2)}) copy-start(bf16[8,128,512]{2,1,0:T(8,128)(2,1)} %wk_hbm.1) | copy-start | bytes 3145732
  3.6 1.2 %copy-start.2 = (bf16[8,512,128]{2,1,0:T(8,128)(2,1)S(1)}, bf16[8,512,128]{2,1,0:T(8,128)(2,1)}, u32[]{:S(2)}) copy-start(bf16[8,512,128]{2,1,0:T(8,128)(2,1)} %wv_hbm.1) | copy-start | bytes 3145732
  4.9 0.9 copy-start.3
  5.8 0.7 copy-start.4
  6.5 0.7 copy-start.5
  7.1 0.7 copy-start.6

commit v2 on v1

v2 whole, which is shorter than its diff:
```python
import functools

import jax
import jax.numpy as jnp
import numpy as np
from jax import lax
from jax.experimental import pallas as pl
from jax.experimental.pallas import tpu as pltpu
from jax.sharding import PartitionSpec as P

LAT = 512
ROPE = 64
NOPE = 128
VDIM = 128
BLK = 64
TILE = 16
LMAX = 4
NEG = -1e30
PARTS = 4
LOG2E = 1.4426950408889634
MESH = pl.DeviceIdType.MESH
F32 = jnp.float32
BF16 = jnp.bfloat16


def dot_nt(a, b):
    return lax.dot_general(a, b, (((1,), (1,)), ((), ())), preferred_element_type=F32)


def dot_nn(a, b):
    return jnp.dot(a, b, preferred_element_type=F32)


def kernel(
    sizes,
    ql_hbm, wq_hbm, wr_hbm, wk_hbm, wv_hbm, wo_hbm, cache_hbm,
    lists_hbm, counts_hbm, pos_hbm, freq_hbm,
    out_ref,
    ql, wq, wr, wk, wv, wo, cache, rope_key,
    lists_ref, counts_ref, pos_ref, freq_ref, scal, scal_smem, posbuf,
    qrecv, qabs, kstage, nabs,
    psend, precv, ssend, srecv, coef, vown, vall, osend, orecv,
    in_sem, ex_ss, ex_rs, scal_sem,
    q_ss, q_rs, r_ss, p_ss, p_rs, s_ss, s_rs, v_ss, v_rs, o_ss, o_rs,
):
    n_ctx, n_head, heads, tok, blocks, maxb, tiles, parts = sizes
    peers = n_ctx // 2
    n_y = peers // 2
    me_h = lax.axis_index("head")
    me_c = lax.axis_index("ctx")
    me8 = me_c // 2
    core = me_c % 2
    me_y = me8 // 2
    me_x = me8 % 2
    me_z = me_h // 2
    lo = me_h % 2
    sibling = (me_h, me8 * 2 + (1 - core))
    across = (me_z * 2 + (1 - lo), me_c)
    nope_w = heads * NOPE
    rope_w = heads * ROPE
    tiles_src = tok // TILE
    tiles_part = tiles_src // parts
    tok_part = tok // parts
    rows = heads * TILE
    keys = 2 * LMAX * BLK

    def shift_of(pair, g):
        middle = ((pair + 1) // 2) % 2
        dx = middle * (pair // 2) + (1 - middle) * g
        dy = middle * (3 - 2 * g) + (1 - middle) * 2 * (pair // 3)
        return dy, dx

    def peer8(pair, g):
        dy, dx = shift_of(pair, g)
        return ((me_y + dy) % n_y) * 2 + (me_x + dx) % 2

    def peer(pair, g):
        return (me_h, peer8(pair, g) * 2 + core)

    def mirror(pair, g):
        middle = ((pair + 1) // 2) % 2
        return 2 * pair + middle * (1 - g) + (1 - middle) * g

    small = [
        pltpu.make_async_copy(pos_hbm, pos_ref, in_sem.at[7]),
        pltpu.make_async_copy(freq_hbm, freq_ref, in_sem.at[8]),
        pltpu.make_async_copy(lists_hbm, lists_ref, in_sem.at[9]),
        pltpu.make_async_copy(counts_hbm, counts_ref, in_sem.at[10]),
    ]
    loads = [
        pltpu.make_async_copy(ql_hbm, ql, in_sem.at[0]),
        pltpu.make_async_copy(wq_hbm, wq, in_sem.at[1]),
        pltpu.make_async_copy(wr_hbm, wr, in_sem.at[2]),
        pltpu.make_async_copy(
            cache_hbm, cache.at[pl.ds(core * blocks, blocks)], in_sem.at[3]
        ),
        pltpu.make_async_copy(wk_hbm, wk, in_sem.at[4]),
        pltpu.make_async_copy(wv_hbm, wv, in_sem.at[5]),
        pltpu.make_async_copy(wo_hbm, wo.at[0, core], in_sem.at[6]),
    ]
    for load in small + loads:
        load.start()

    barrier = pltpu.get_barrier_semaphore()

    def greet(device):
        pl.semaphore_signal(barrier, inc=1, device_id=device, device_id_type=MESH)

    def greet_peers(pair, carry):
        for g in range(2):

            @pl.when(2 * pair + g != 0)
            def _():
                greet(peer(pair, g))

        return carry

    def value_source(n, other):
        return (me_z * 2 + other, (n * 2 + core) * 2 + lo)

    def greet_value_sources(n, carry):
        for other in range(2):

            @pl.when((n != me_y) | (other != lo) | (core != me_x) | (lo != core))
            def _():
                greet(value_source(n, other))

        return carry

    def greet_planes(n, carry):
        @pl.when((n != me_z) | (me_z % 2 != core))
        def _():
            greet((n * 2 + lo, me8 * 2 + me_z % 2))

        return carry

    greet(sibling)
    greet(across)
    lax.fori_loop(0, peers // 2, greet_peers, 0)
    lax.fori_loop(0, n_y, greet_value_sources, 0)
    lax.fori_loop(0, peers, greet_planes, 0)

    small[0].wait()
    small[1].wait()
    pos_row = pos_ref[pl.ds(me8, 1), :].astype(F32)
    posbuf[...] = jnp.transpose(jnp.broadcast_to(pos_row, (128, 128)))
    pos_col = posbuf[pl.ds(pl.multiple_of(core * tok, tok), tok), :]
    angle = pos_col * freq_ref[...]
    cosine = jnp.cos(angle)
    lane = lax.broadcasted_iota(jnp.int32, (tok, 128), 1)
    first_half = (lane % ROPE) < (ROPE // 2)
    sine = jnp.where(first_half, -jnp.sin(angle), jnp.sin(angle))

    loads[0].wait()
    loads[1].wait()
    latent = ql[...]
    chunk = 512
    for start in range(0, nope_w, chunk):
        qrecv[0, :, start : start + chunk] = dot_nn(
            latent, wq[:, start : start + chunk]
        ).astype(BF16)
    loads[2].wait()
    rope_part = dot_nn(latent, wr[...])
    for start in range(0, rope_w, 128):
        part = rope_part[:, start : start + 128]
        swapped = jnp.where(
            first_half,
            pltpu.roll(part, 128 - ROPE // 2, 1),
            pltpu.roll(part, ROPE // 2, 1),
        )
        qrecv[0, :, nope_w + start : nope_w + start + 128] = (
            part * cosine + swapped * sine
        ).astype(BF16)

    small[2].wait()
    small[3].wait()
    counts = counts_ref[...]
    zero = jnp.zeros((1, tiles), jnp.int32)
    found = [zero, zero]
    index = [[zero] * LMAX, [zero] * LMAX]
    for slot in range(maxb):
        entry = lists_ref[slot : slot + 1, :]
        shard = entry % n_ctx
        local = entry // n_ctx
        valid = counts > slot
        for e in range(2):
            here = valid & (shard == me8 * 2 + e)
            for j in range(LMAX):
                index[e][j] = jnp.where(here & (found[e] == j), local + e * blocks, index[e][j])
            found[e] = found[e] + jnp.where(here, 1, 0)
    scal[...] = jnp.zeros_like(scal)
    for e in range(2):
        for j in range(LMAX):
            scal[e * LMAX + j : e * LMAX + j + 1, 0:tiles] = index[e][j]
        scal[2 * LMAX + e : 2 * LMAX + e + 1, 0:tiles] = found[e]
    scal_copy = pltpu.make_async_copy(scal, scal_smem, scal_sem)
    scal_copy.start()

    loads[3].wait()

    def double_key(b, carry):
        part = cache[core * blocks + b, :, LAT : LAT + ROPE]
        rope_key[core * blocks + b] = jnp.concatenate([part, part], axis=1)
        return carry

    lax.fori_loop(0, blocks, double_key, 0)

    scal_copy.wait()
    self_value = (1 - (core + lo) % 2) * (1 - (core + me_x) % 2)
    self_plane = 1 - (me_z + core) % 2
    pl.semaphore_wait(barrier, peers - 1 + 2 + peers - self_value + peers - self_plane)

    def remote(src, dst, send_sem, recv_sem, device):
        return pltpu.make_async_remote_copy(
            src_ref=src,
            dst_ref=dst,
            send_sem=send_sem,
            recv_sem=recv_sem,
            device_id=device,
            device_id_type=MESH,
        )

    def q_copy(held, pair, g, slot, send_sem):
        return remote(qrecv.at[held], qrecv.at[slot], send_sem, q_rs.at[slot], peer(pair, g))

    first_q = [q_copy(0, 0, 1, 1, q_ss.at[0])]
    relay_q = []
    last_q = []
    if n_y == 4:
        first_q += [q_copy(0, 1, g, mirror(1, g), q_ss.at[1 + g]) for g in range(2)]
        relay_q = [q_copy(1, 1, g, mirror(2, g), r_ss.at[g]) for g in range(2)]
        last_q = [
            q_copy(2 + me_x, 1, 1 - me_x, 6, r_ss.at[2]),
            q_copy(5 - me_x, 1, me_x, 7, r_ss.at[3]),
        ]
    for copy in first_q:
        copy.start()

    def exchange(which, src, dst, device):
        return remote(src, dst, ex_ss.at[which], ex_rs.at[which], device)

    def exchanges(side):
        half = pl.ds(side * blocks, blocks)
        own = pl.ds(core * blocks, blocks)
        return [
            exchange(0, cache_hbm, cache.at[half], sibling),
            exchange(1, rope_key.at[own], rope_key.at[half], sibling),
            exchange(2, wo_hbm, wo.at[0, side], sibling),
            exchange(3, wo_hbm, wo.at[1, core], across),
            exchange(4, wo.at[1, core], wo.at[1, side], sibling),
        ]

    swaps_out = exchanges(core)
    swaps_in = exchanges(1 - core)
    swaps_in[3] = swaps_out[3]
    for swap in swaps_out[:3]:
        swap.start()

    pairs = peers // 2
    seats = min(2, pairs)
    half_lane = lax.broadcasted_iota(jnp.int32, (1, 128), 1)
    half_mask = [
        (half_lane < ROPE).astype(F32).astype(BF16),
        (half_lane >= ROPE).astype(F32).astype(BF16),
    ]
    key_lane = lax.broadcasted_iota(jnp.int32, (1, keys), 1)
    key_slot = key_lane // BLK
    stat_lane = lax.broadcasted_iota(jnp.int32, (rows, 128), 1)
    scale = LOG2E * (NOPE + ROPE) ** (-0.5)

    loads[4].wait()

    def absorb(pair):
        group, first = 2, 2 * pair
        span = pl.ds(first, group)
        spot = pl.ds(pl.multiple_of(first * tok, tok), group * tok)
        for h in range(heads):
            nope = qrecv[span, :, h * NOPE : (h + 1) * NOPE].reshape(group * tok, NOPE)
            qabs[h, spot, 0:LAT] = dot_nn(nope, wk[h]).astype(BF16)
            start = nope_w + (h // 2) * 128
            pair = qrecv[span, :, start : start + 128].reshape(group * tok, 128)
            qabs[h, spot, LAT : LAT + 128] = pair * half_mask[h % 2]

    def attend(pair, part, seat):
        for g in range(2):
            slot = 2 * pair + g
            src = peer8(pair, g) * 2 + core
            stats = jnp.zeros((rows, 128), F32)
            for i in range(tiles_part):
                tile = src * tiles_src + part * tiles_part + i
                stage = (2 * seat + g) * tiles_part + i
                for j in range(2 * LMAX):
                    block = scal_smem[j, tile]
                    kstage[stage, j * BLK : (j + 1) * BLK, 0:LAT] = cache[block, :, 0:LAT]
                    kstage[stage, j * BLK : (j + 1) * BLK, LAT : LAT + 128] = rope_key[block]
                live_even = scal_smem[2 * LMAX, tile]
                live_odd = scal_smem[2 * LMAX + 1, tile]
                limit = jnp.where(key_slot < LMAX, live_even, live_odd + LMAX)
                bias = jnp.where(key_slot < limit, 0.0, NEG)
                start = pl.multiple_of(slot * tok + part * tok_part + i * TILE, TILE)
                query = qabs[:, pl.ds(start, TILE), :].reshape(rows, LAT + 128)
                score = dot_nt(query, kstage[stage]) * scale + bias
                peak = jnp.max(score, axis=1, keepdims=True)
                weight = jnp.exp2(score - peak)
                total = jnp.sum(weight, axis=1, keepdims=True)
                number = dot_nn(weight.astype(BF16), kstage[stage, :, 0:LAT])
                place = (2 * seat + g) * tok_part + i * TILE
                nabs[:, place : place + TILE, :] = number.astype(BF16).reshape(heads, TILE, LAT)
                stats = jnp.where(stat_lane == i, peak, stats)
                stats = jnp.where(stat_lane == tiles_part + i, total, stats)
            ssend[part, slot] = jnp.transpose(stats)[0:8, :]

    def p_copy(part, pair, g, slot):
        held = 2 * pair + g
        return remote(
            psend.at[part, held], precv.at[part, slot],
            p_ss.at[part, held], p_rs.at[part, slot], peer(pair, g),
        )

    def s_copy(part, pair, g, slot):
        held = 2 * pair + g
        return remote(
            ssend.at[part, held], srecv.at[part, slot],
            s_ss.at[part, held], s_rs.at[part, slot], peer(pair, g),
        )

    def send_values(pair, part, seats, seat):
        start = 2 * seat * tok_part
        count = 2 * seats * tok_part
        for h in range(heads):
            value = dot_nn(nabs[h, start : start + count], wv[h]).astype(BF16)
            for n in range(2 * seats):
                psend[part, 2 * pair + n, h] = value[n * tok_part : (n + 1) * tok_part, :]
        for n in range(2 * seats):
            now, g = pair + n // 2, n % 2

            @pl.when(2 * now + g != 0)
            def _():
                s_copy(part, now, g, mirror(now, g)).start()
                p_copy(part, now, g, mirror(now, g)).start()

    def q_wait(slot):
        q_copy(0, 0, 1, slot, q_ss.at[0]).wait_recv()

    def attend_new(pair, carry):
        for g in range(2):

            @pl.when(2 * pair + g != 0)
            def _():
                q_wait(2 * pair + g)

        @pl.when(pair == 0)
        def _():
            for copy in relay_q:
                copy.start()
            swaps_out[3].start()

        if n_y == 4:

            @pl.when(pair == 1)
            def _():
                last_q[0].start()

            @pl.when(pair == 2)
            def _():
                last_q[1].start()

        absorb(pair)

        @pl.when(pair == 0)
        def _():
            loads[5].wait()
            swaps_in[0].wait_recv()
            swaps_in[1].wait_recv()

        for part in range(2):
            attend(pair, part, part)
        for part in range(2):
            send_values(pair, part, 1, part)
        return carry

    def attend_again(part, seats):
        def step(n, carry):
            first = pairs - (n + 1) * seats
            for seat in range(seats):
                attend(first + seat, part, seat)
            send_values(first, part, seats, 0)
            return carry

        return step

    def combine(part):
        def p_wait(slot, carry):
            s_copy(part, 0, 0, slot).wait_recv()
            p_copy(part, 0, 0, slot).wait_recv()
            return carry

        lax.fori_loop(1, peers, p_wait, 0)
        srecv[part, 0] = ssend[part, 0]
        peaks = srecv[part, :, 0:tiles_part, :]
        sums = srecv[part, :, tiles_part : 2 * tiles_part, :]
        top = jnp.max(peaks, axis=0, keepdims=True)
        share = jnp.exp2(peaks - top)
        share = share / jnp.sum(share * sums, axis=0, keepdims=True)
        coef[...] = jnp.zeros_like(coef)
        for src in range(peers):
            coef[src * tiles_part : (src + 1) * tiles_part, :] = share[src]
        coef_t = jnp.transpose(coef[...])
        for i in range(tiles_part):
            mixed = jnp.zeros((rows, VDIM), F32)
            for src in range(peers):
                column = coef_t[:, src * tiles_part + i : src * tiles_part + i + 1]
                held = psend if src == 0 else precv
                term = held[part, src, :, i * TILE : (i + 1) * TILE, :].astype(F32)
                mixed = mixed + column * term.reshape(rows, VDIM)
            mixed = mixed.astype(BF16).reshape(heads, TILE, VDIM)
            for h in range(heads):
                vown[part, i * TILE : (i + 1) * TILE, h * VDIM : (h + 1) * VDIM] = mixed[h]

    def v_copy(part, n, slot):
        target = ((me_y + n // 2) % n_y) * 2 + (me_x + n) % 2
        return remote(
            vown.at[part], vall.at[part, slot // n_y, slot % n_y],
            v_ss.at[part, n], v_rs.at[part, slot],
            (me_z * 2 + core, target * 2 + me_x),
        )

    my_slot = lo * n_y + me_y

    def keeps(n):
        return (n == 0) & (core == lo) & (core == me_x)

    def gather(part):
        def v_start(n, carry):
            @pl.when(keeps(n))
            def _():
                vall[part, lo, me_y] = vown[part]

            @pl.when(jnp.logical_not(keeps(n)))
            def _():
                v_copy(part, n, my_slot).start()

            return carry

        lax.fori_loop(0, peers, v_start, 0)

    def o_copy(part, n, e, slot):
        plane = 2 * n + core
        return remote(
            osend.at[part, n, e], orecv.at[part, slot],
            o_ss.at[part, n, e], o_rs.at[part, slot],
            (plane * 2 + lo, me8 * 2 + e),
        )

    def stays(n, e):
        return (2 * n + core == me_z) & (core == e)

    def project(part):
        def v_wait(slot, carry):
            @pl.when(
                (slot != my_slot) | (core != lo) | (core != me_x)
            )
            def _():
                v_copy(part, 0, slot).wait_recv()

            return carry

        lax.fori_loop(0, peers, v_wait, 0)
        for e in range(2):
            product = dot_nt(vall[part, lo].reshape(n_y * tok_part, nope_w), wo[0, e])
            product = product + dot_nt(
                vall[part, 1 - lo].reshape(n_y * tok_part, nope_w), wo[1, e]
            )
            product = product.astype(BF16)
            for n in range(n_y):
                osend[part, n, e] = product[n * tok_part : (n + 1) * tok_part, :]

        def o_start(n, carry):
            at = (n + me_z // 2) % n_y
            for e in range(2):

                @pl.when(stays(at, e))
                def _():
                    orecv[part, me_z] = osend[part, at, e]

                @pl.when(jnp.logical_not(stays(at, e)))
                def _():
                    o_copy(part, at, e, me_z).start()

            return carry

        lax.fori_loop(0, n_y, o_start, 0)

    def collect(part):
        @pl.when(me_z % 2 != core)
        def _():
            o_copy(part, 0, 0, me_z).wait_recv()

        total = orecv[part, me_z].astype(F32)

        def add_plane(n, total):
            src = (me_z + n) % peers
            o_copy(part, 0, 0, src).wait_recv()
            return total + orecv[part, src].astype(F32)

        total = lax.fori_loop(1, peers, add_plane, total)
        out_ref[part * tok_part : (part + 1) * tok_part, :] = total.astype(BF16)

    lax.fori_loop(0, pairs, attend_new, 0)
    lax.fori_loop(0, pairs // seats, attend_again(2, seats), 0)
    for part in range(2):
        combine(part)
        gather(part)
    lax.fori_loop(0, pairs // seats, attend_again(3, seats), 0)
    combine(2)
    gather(2)
    loads[6].wait()
    swaps_in[2].wait_recv()
    swaps_in[3].wait_recv()
    swaps_out[4].start()
    swaps_in[4].wait_recv()
    project(0)
    project(1)
    combine(3)
    gather(3)
    project(2)
    project(3)
    for part in range(parts):
        collect(part)

    for swap in swaps_out:
        swap.wait_send()

    for copy in first_q + relay_q + last_q:
        copy.wait_send()

    def drain_peers(pair, carry):
        for g in range(2):

            @pl.when(2 * pair + g != 0)
            def _():
                for part in range(parts):
                    p_copy(part, pair, g, 0).wait_send()
                    s_copy(part, pair, g, 0).wait_send()

        return carry

    lax.fori_loop(0, pairs, drain_peers, 0)

    def drain_values(n, carry):
        @pl.when(jnp.logical_not(keeps(n)))
        def _():
            for part in range(parts):
                v_copy(part, n, my_slot).wait_send()

        return carry

    lax.fori_loop(0, peers, drain_values, 0)

    def drain_planes(n, carry):
        for e in range(2):

            @pl.when(jnp.logical_not(stays(n, e)))
            def _():
                for part in range(parts):
                    o_copy(part, n, e, me_z).wait_send()

        return carry

    lax.fori_loop(0, n_y, drain_planes, 0)


def local(
    n_ctx, n_head,
    query_latent, w_query_nope, w_query_rope, w_absorb_key, w_absorb_value, w_output,
    latent_cache, block_lists, block_counts, positions,
):
    tok, q_lat = query_latent.shape
    heads = w_absorb_key.shape[0]
    blocks = latent_cache.shape[0]
    tiles, maxb = block_lists.shape
    cols = w_output.shape[1]
    peers = n_ctx // 2
    tiles_src = tok // TILE
    nope_w = heads * NOPE
    rope_w = heads * ROPE
    rows = heads * TILE
    keys = 2 * LMAX * BLK
    half = ROPE // 2
    frequency = 10000.0 ** (-2.0 * np.arange(half, dtype=np.float64) / ROPE)
    frequency = np.tile(frequency.astype(np.float32), 128 // half)[None, :]
    parts = PARTS
    n_y = peers // 2
    tok_part = tok // parts
    sizes = (n_ctx, n_head, heads, tok, blocks, maxb, tiles, parts)
    hbm = pl.BlockSpec(memory_space=pltpu.HBM)
    vmem = pl.BlockSpec(memory_space=pltpu.VMEM)
    dma = pltpu.SemaphoreType.DMA
    return pl.pallas_call(
        functools.partial(kernel, sizes),
        out_shape=jax.ShapeDtypeStruct((tok, cols), BF16),
        in_specs=[hbm] * 11,
        out_specs=vmem,
        scratch_shapes=[
            pltpu.VMEM((tok, q_lat), BF16),
            pltpu.VMEM((q_lat, nope_w), BF16),
            pltpu.VMEM((q_lat, rope_w), BF16),
            pltpu.VMEM((heads, NOPE, LAT), BF16),
            pltpu.VMEM((heads, LAT, VDIM), BF16),
            pltpu.VMEM((2, 2, cols, heads * VDIM), BF16),
            pltpu.VMEM((2 * blocks, BLK, LAT + ROPE), BF16),
            pltpu.VMEM((2 * blocks, BLK, 128), BF16),
            pltpu.VMEM((maxb, tiles), jnp.int32),
            pltpu.VMEM((1, tiles), jnp.int32),
            pltpu.VMEM((positions.shape[0] // 128, 128), jnp.int32),
            pltpu.VMEM((1, 128), F32),
            pltpu.VMEM((16, 128), jnp.int32),
            pltpu.SMEM((16, 128), jnp.int32),
            pltpu.VMEM((128, 128), F32),
            pltpu.VMEM((peers, tok, nope_w + rope_w), BF16),
            pltpu.VMEM((heads, peers * tok, LAT + 128), BF16),
            pltpu.VMEM((4 * tiles_src // parts, keys, LAT + 128), BF16),
            pltpu.VMEM((heads, 4 * tok_part, LAT), BF16),
            pltpu.VMEM((parts, peers, heads, tok_part, VDIM), BF16),
            pltpu.VMEM((parts, peers, heads, tok_part, VDIM), BF16),
            pltpu.VMEM((parts, peers, 8, 128), F32),
            pltpu.VMEM((parts, peers, 8, 128), F32),
            pltpu.VMEM((128, 128), F32),
            pltpu.VMEM((parts, tok_part, nope_w), BF16),
            pltpu.VMEM((parts, 2, n_y, tok_part, nope_w), BF16),
            pltpu.VMEM((parts, n_y, 2, tok_part, cols), BF16),
            pltpu.VMEM((parts, peers, tok_part, cols), BF16),
            dma((11,)),
            dma((5,)),
            dma((5,)),
            dma(()),
            dma((3,)),
            dma((peers,)),
            dma((4,)),
            dma((parts, peers)),
            dma((parts, peers)),
            dma((parts, peers)),
            dma((parts, peers)),
            dma((parts, peers)),
            dma((parts, peers)),
            dma((parts, n_y, 2)),
            dma((parts, peers)),
        ],
        compiler_params=pltpu.CompilerParams(
            collective_id=0, has_side_effects=True, vmem_limit_bytes=63 * 1024 * 1024
        ),
    )(
        query_latent, w_query_nope, w_query_rope, w_absorb_key, w_absorb_value, w_output.T,
        latent_cache, block_lists.T, block_counts.reshape(1, tiles),
        positions.reshape(positions.shape[0] // 128, 128), jnp.asarray(frequency),
    )


def solution(mesh):
    in_specs = (
        P("ctx", None),
        P(None, "head"),
        P(None, "head"),
        P("head", None, None),
        P("head", None, None),
        P("head", "ctx"),
        P(None, "ctx", None),
        P(),
        P(),
        P(),
    )
    run = functools.partial(local, mesh.shape["ctx"], mesh.shape["head"])
    return jax.shard_map(
        run, mesh=mesh, in_specs=in_specs, out_specs=P("head", "ctx"), check_vma=False
    )
```

time: 113 us -> 82.1 us (0.73)
  the two profiles are of different devices: /device:TPU:10 before, /device:TPU:1 now
where the time goes in v2:
time: 82.1 us; the launch traced here: 80.9 us
  Pallas kernels  79.4 us (97%)
  local copies, waits for them, and re-layouts  1.47 us (2%)
    pallas_call x1, Pallas kernels, local(): pl.pallas_call(functools.partial(kernel, sizes), out_shape=jax.ShapeDtype...  79.4 us

profile of v2, /device:TPU:1, one launch (start us, length us, event | category | flops | bytes accessed | tf_op | source)
XLA Modules:
  0.0 80.9 jit_solution(6893359620268388337)
XLA Ops:
  0.0 79.4 %shard_map.109 = bf16[64,448]{1,0:T(8,128)(2,1)} custom-call(bf16[64,1536]{1,0:T(8,128)(2,1)} %ql_hbm.1, bf16[1536,1024]{1,0:T(8,128)(2,1)} %wq_hbm.1, bf16[1536,512]{1,0:T(8,128)(2,1)} %wr_hbm.1, bf16[8,128,512]{2,1,0:T(8,128)(2,1)} %wk_hbm.1, bf16[8,512,128]{2,1,0:T(8,128)(2,1)} %wv_hbm.1, bf16[448,1024]{1,0:T(8,128)(2,1)} %bitcast.4, ...), custom_call_target="tpu_custom_call" | custom-call | tf_op jit(solution)/shard_map/pallas_call | solution.py:599
  79.4 1.5 %copy.13 = bf16[64,448]{1,0:T(8,128)(2,1)} copy(bf16[64,448]{1,0:T(8,128)(2,1)} %shard_map.109) | data formatting | bytes 114688

commit v3 on v2

--- a/solution.py
+++ b/solution.py
@@ -253,7 +253,7 @@
     swaps_out = exchanges(core)
     swaps_in = exchanges(1 - core)
     swaps_in[3] = swaps_out[3]
-    for swap in swaps_out[:3]:
+    for swap in swaps_out[:4]:
         swap.start()
 
     pairs = peers // 2
@@ -308,7 +308,7 @@
                 nabs[:, place : place + TILE, :] = number.astype(BF16).reshape(heads, TILE, LAT)
                 stats = jnp.where(stat_lane == i, peak, stats)
                 stats = jnp.where(stat_lane == tiles_part + i, total, stats)
-            ssend[part, slot] = jnp.transpose(stats)[0:8, :]
+            ssend[part, slot] = jnp.transpose(stats)[0 : 2 * tiles_part, :]
 
     def p_copy(part, pair, g, slot):
         held = 2 * pair + g
@@ -324,20 +324,21 @@
             s_ss.at[part, held], s_rs.at[part, slot], peer(pair, g),
         )
 
-    def send_values(pair, part, seats, seat):
-        start = 2 * seat * tok_part
-        count = 2 * seats * tok_part
+    def send_values(held):
+        width = 2 * tok_part
         for h in range(heads):
-            value = dot_nn(nabs[h, start : start + count], wv[h]).astype(BF16)
-            for n in range(2 * seats):
-                psend[part, 2 * pair + n, h] = value[n * tok_part : (n + 1) * tok_part, :]
-        for n in range(2 * seats):
-            now, g = pair + n // 2, n % 2
-
-            @pl.when(2 * now + g != 0)
-            def _():
-                s_copy(part, now, g, mirror(now, g)).start()
-                p_copy(part, now, g, mirror(now, g)).start()
+            value = dot_nn(nabs[h, 0 : len(held) * width], wv[h]).astype(BF16)
+            for seat, (pair, part) in enumerate(held):
+                for g in range(2):
+                    start = seat * width + g * tok_part
+                    psend[part, 2 * pair + g, h] = value[start : start + tok_part, :]
+        for pair, part in held:
+            for g in range(2):
+
+                @pl.when(2 * pair + g != 0)
+                def _():
+                    s_copy(part, pair, g, mirror(pair, g)).start()
+                    p_copy(part, pair, g, mirror(pair, g)).start()
 
     def q_wait(slot):
         q_copy(0, 0, 1, slot, q_ss.at[0]).wait_recv()
@@ -353,7 +354,6 @@
         def _():
             for copy in relay_q:
                 copy.start()
-            swaps_out[3].start()
 
         if n_y == 4:
 
@@ -375,16 +375,16 @@
 
         for part in range(2):
             attend(pair, part, part)
-        for part in range(2):
-            send_values(pair, part, 1, part)
+        send_values([(pair, part) for part in range(2)])
         return carry
 
     def attend_again(part, seats):
         def step(n, carry):
             first = pairs - (n + 1) * seats
-            for seat in range(seats):
-                attend(first + seat, part, seat)
-            send_values(first, part, seats, 0)
+            held = [(first + seat, part) for seat in range(seats)]
+            for seat, (pair, _) in enumerate(held):
+                attend(pair, part, seat)
+            send_values(held)
             return carry
 
         return step
@@ -455,41 +455,44 @@
     def stays(n, e):
         return (2 * n + core == me_z) & (core == e)
 
-    def project(part):
+    def project(first, count):
         def v_wait(slot, carry):
-            @pl.when(
-                (slot != my_slot) | (core != lo) | (core != me_x)
-            )
-            def _():
-                v_copy(part, 0, slot).wait_recv()
+            @pl.when((slot != my_slot) | (core != lo) | (core != me_x))
+            def _():
+                for part in range(first, first + count):
+                    v_copy(part, 0, slot).wait_recv()
 
             return carry
 
         lax.fori_loop(0, peers, v_wait, 0)
+        size = count * n_y * tok_part
+        span = slice(first, first + count)
         for e in range(2):
-            product = dot_nt(vall[part, lo].reshape(n_y * tok_part, nope_w), wo[0, e])
-            product = product + dot_nt(
-                vall[part, 1 - lo].reshape(n_y * tok_part, nope_w), wo[1, e]
-            )
+            product = dot_nt(vall[span, lo].reshape(size, nope_w), wo[0, e])
+            product = product + dot_nt(vall[span, 1 - lo].reshape(size, nope_w), wo[1, e])
             product = product.astype(BF16)
-            for n in range(n_y):
-                osend[part, n, e] = product[n * tok_part : (n + 1) * tok_part, :]
-
-        def o_start(n, carry):
-            at = (n + me_z // 2) % n_y
-            for e in range(2):
-
-                @pl.when(stays(at, e))
-                def _():
-                    orecv[part, me_z] = osend[part, at, e]
-
-                @pl.when(jnp.logical_not(stays(at, e)))
-                def _():
-                    o_copy(part, at, e, me_z).start()
-
-            return carry
-
-        lax.fori_loop(0, n_y, o_start, 0)
+            for k in range(count):
+                for n in range(n_y):
+                    start = (k * n_y + n) * tok_part
+                    osend[first + k, n, e] = product[start : start + tok_part, :]
+
+        for part in range(first, first + count):
+
+            def o_start(n, carry):
+                at = (n + me_z // 2) % n_y
+                for e in range(2):
+
+                    @pl.when(stays(at, e))
+                    def _():
+                        orecv[part, me_z] = osend[part, at, e]
+
+                    @pl.when(jnp.logical_not(stays(at, e)))
+                    def _():
+                        o_copy(part, at, e, me_z).start()
+
+                return carry
+
+            lax.fori_loop(0, n_y, o_start, 0)
 
     def collect(part):
         @pl.when(me_z % 2 != core)
@@ -507,11 +510,13 @@
         out_ref[part * tok_part : (part + 1) * tok_part, :] = total.astype(BF16)
 
     lax.fori_loop(0, pairs, attend_new, 0)
-    lax.fori_loop(0, pairs // seats, attend_again(2, seats), 0)
+    lax.fori_loop(0, 1, attend_again(2, pairs), 0)
+    half = (pairs // seats + 1) // 2
+    lax.fori_loop(0, half, attend_again(3, seats), 0)
     for part in range(2):
         combine(part)
         gather(part)
-    lax.fori_loop(0, pairs // seats, attend_again(3, seats), 0)
+    lax.fori_loop(half, pairs // seats, attend_again(3, seats), 0)
     combine(2)
     gather(2)
     loads[6].wait()
@@ -519,12 +524,11 @@
     swaps_in[3].wait_recv()
     swaps_out[4].start()
     swaps_in[4].wait_recv()
-    project(0)
-    project(1)
+    project(0, 2)
     combine(3)
     gather(3)
-    project(2)
-    project(3)
+    project(2, 1)
+    project(3, 1)
     for part in range(parts):
         collect(part)
 
@@ -619,12 +623,12 @@
             pltpu.VMEM((128, 128), F32),
             pltpu.VMEM((peers, tok, nope_w + rope_w), BF16),
             pltpu.VMEM((heads, peers * tok, LAT + 128), BF16),
-            pltpu.VMEM((4 * tiles_src // parts, keys, LAT + 128), BF16),
-            pltpu.VMEM((heads, 4 * tok_part, LAT), BF16),
+            pltpu.VMEM((max(4, peers) * tiles_src // parts, keys, LAT + 128), BF16),
+            pltpu.VMEM((heads, max(4, peers) * tok_part, LAT), BF16),
             pltpu.VMEM((parts, peers, heads, tok_part, VDIM), BF16),
             pltpu.VMEM((parts, peers, heads, tok_part, VDIM), BF16),
-            pltpu.VMEM((parts, peers, 8, 128), F32),
-            pltpu.VMEM((parts, peers, 8, 128), F32),
+            pltpu.VMEM((parts, peers, 2 * tiles_src // parts, 128), F32),
+            pltpu.VMEM((parts, peers, 2 * tiles_src // parts, 128), F32),
             pltpu.VMEM((128, 128), F32),
             pltpu.VMEM((parts, tok_part, nope_w), BF16),
             pltpu.VMEM((parts, 2, n_y, tok_part, nope_w), BF16),

time: 82.1 us -> 78.3 us (0.954); the launches traced: 80.9 us -> 78.2 us
  Pallas kernels: 79.4 us -> 76.7 us
    pallas_call x1, Pallas kernels: 79.4 us -> 76.7 us  [local(): pl.pallas_call(functools.partial(kernel, sizes), out_shape=jax.ShapeDtype...]
where the time goes in v3:
time: 78.3 us; the launch traced here: 78.2 us
  Pallas kernels  76.7 us (98%)
  local copies, waits for them, and re-layouts  1.47 us (2%)
    pallas_call x1, Pallas kernels, local(): pl.pallas_call(functools.partial(kernel, sizes), out_shape=jax.ShapeDtype...  76.7 us

profile of v3, /device:TPU:1, one launch (start us, length us, event | category | flops | bytes accessed | tf_op | source)
XLA Modules:
  0.0 78.2 jit_solution(8246001172615175136)
XLA Ops:
  0.0 76.7 %shard_map.109 = bf16[64,448]{1,0:T(8,128)(2,1)} custom-call(bf16[64,1536]{1,0:T(8,128)(2,1)} %ql_hbm.1, bf16[1536,1024]{1,0:T(8,128)(2,1)} %wq_hbm.1, bf16[1536,512]{1,0:T(8,128)(2,1)} %wr_hbm.1, bf16[8,128,512]{2,1,0:T(8,128)(2,1)} %wk_hbm.1, bf16[8,512,128]{2,1,0:T(8,128)(2,1)} %wv_hbm.1, bf16[448,1024]{1,0:T(8,128)(2,1)} %bitcast.4, ...), custom_call_target="tpu_custom_call" | custom-call | tf_op jit(solution)/shard_map/pallas_call | solution.py:603
  76.7 1.5 %copy.13 = bf16[64,448]{1,0:T(8,128)(2,1)} copy(bf16[64,448]{1,0:T(8,128)(2,1)} %shard_map.109) | data formatting | bytes 114688

commit v4 on v3

--- a/solution.py
+++ b/solution.py
@@ -431,7 +431,9 @@
         return (n == 0) & (core == lo) & (core == me_x)
 
     def gather(part):
-        def v_start(n, carry):
+        def v_start(step, carry):
+            n = (step + peers // 2) % peers
+
             @pl.when(keeps(n))
             def _():
                 vall[part, lo, me_y] = vown[part]
@@ -479,7 +481,7 @@
         for part in range(first, first + count):
 
             def o_start(n, carry):
-                at = (n + me_z // 2) % n_y
+                at = (n + me_z // 2 + n_y // 2) % n_y
                 for e in range(2):
 
                     @pl.when(stays(at, e))

time: 78.3 us -> 77.9 us (level)
  no operation moved by 1% of the time
where the time goes in v4:
time: 77.9 us; the launch traced here: 77.7 us
  Pallas kernels  76.3 us (98%)
  local copies, waits for them, and re-layouts  1.47 us (2%)
    pallas_call x1, Pallas kernels, local(): pl.pallas_call(functools.partial(kernel, sizes), out_shape=jax.ShapeDtype...  76.3 us

profile of v4, /device:TPU:1, one launch (start us, length us, event | category | flops | bytes accessed | tf_op | source)
XLA Modules:
  0.0 77.7 jit_solution(6256712636418803158)
XLA Ops:
  0.0 76.3 %shard_map.109 = bf16[64,448]{1,0:T(8,128)(2,1)} custom-call(bf16[64,1536]{1,0:T(8,128)(2,1)} %ql_hbm.1, bf16[1536,1024]{1,0:T(8,128)(2,1)} %wq_hbm.1, bf16[1536,512]{1,0:T(8,128)(2,1)} %wr_hbm.1, bf16[8,128,512]{2,1,0:T(8,128)(2,1)} %wk_hbm.1, bf16[8,512,128]{2,1,0:T(8,128)(2,1)} %wv_hbm.1, bf16[448,1024]{1,0:T(8,128)(2,1)} %bitcast.4, ...), custom_call_target="tpu_custom_call" | custom-call | tf_op jit(solution)/shard_map/pallas_call | solution.py:605
  76.3 1.5 %copy.13 = bf16[64,448]{1,0:T(8,128)(2,1)} copy(bf16[64,448]{1,0:T(8,128)(2,1)} %shard_map.109) | data formatting | bytes 114688
